TPU v7x, 512 devices: a whole 4x8x8 slice. The times are simulated.
512 devices in a mesh: dp: 16 (over z_hi, x, core), seq: 32 (over z_lo, y).
Axes of the slice: x: 4, y: 8, z: 8 (z_hi: 2, z_lo: 4; z = z_hi * 4 + z_lo), core: 2. Of those that a mesh axis runs over, the one named last changes fastest.
Arguments:
- tokens: bfloat16 [16, 8192, 1536], P('dp', 'seq'), may hold values from -6 to 6
- cotangent: bfloat16 [16, 8192, 1536], P('dp', 'seq'), may hold values from -6 to 6
- conv_taps: bfloat16 [3, 1536], replicated, may hold values from -3 to 3
- block_mixes: bfloat16 [6, 256, 256], replicated, may hold values from -0.375 to 0.375
- gate_gain: float32 [1536], replicated, may hold values from 0.5 to 2
Outputs:
- input_grad: bfloat16 [16, 8192, 1536], P('dp', 'seq')
- mixes_grad: float32 [6, 256, 256], replicated
- taps_grad: float32 [3, 1536], replicated
- gain_grad: float32 [1536], replicated
All inputs are finite; a program needn't handle non-finite values.
Results may differ from a plain program's by a relative error of at most 0.0076.
Values may be sent and summed in bfloat16 or wider, within the bound.
A program may use at most 64 MiB of HBM per device.

v0:
```python
import math

import jax
import jax.numpy as jnp
from jax import lax
from jax.sharding import PartitionSpec as P


def padded_2(cells, sides, width):
    for axis, dim in sides:
        count = lax.axis_size(axis)
        ends = count - 1
        head = lax.slice_in_dim(cells, 0, width, axis=dim)
        tail = lax.slice_in_dim(cells, cells.shape[dim] - width, cells.shape[dim], axis=dim)
        cells = jnp.concatenate(
            [
                lax.ppermute(tail, axis, [(i, (i + 1) % count) for i in range(ends)]),
                cells,
                lax.ppermute(head, axis, [((i + 1) % count, i) for i in range(ends)]),
            ],
            axis=dim,
        )
    return cells


def partner_2(shard, axis, distance):
    return lax.ppermute(shard, axis, [(i, i ^ 1 << distance) for i in range(lax.axis_size(axis))])


def extend(field):
    return padded_2(field, (("seq", 1),), 1)


def partner(block, level_bit):
    return partner_2(block, "seq", level_bit)


def apply_mix(matrix, block):
    return jnp.einsum("ij,sjd->sid", matrix, block, preferred_element_type=jnp.float32)


def apply_transposed(matrix, block):
    return jnp.einsum("ji,sjd->sid", matrix, block, preferred_element_type=jnp.float32)


def outer_sum(left, right):
    return jnp.einsum("sid,sjd->ij", left, right, preferred_element_type=jnp.float32)


def local(tokens, cotangent, conv_taps, block_mixes, gate_gain):
    local_slabs, block_len, channels = tokens.shape
    top_bit = lax.axis_size("seq").bit_length() - 1
    far_bit = top_bit - 1
    near_bit = 0
    tok_scale = 1.0 / math.sqrt(
        local_slabs * lax.axis_size("dp") * block_len * lax.axis_size("seq")
    )
    mix_scale = 1.0 / math.sqrt(local_slabs * lax.axis_size("dp") * lax.axis_size("seq") * channels)
    tap_weights = conv_taps.astype(jnp.float32)
    padded = extend(tokens)
    conv_out = (
        tap_weights[0] * padded[:, :-2]
        + tap_weights[1] * padded[:, 1:-1]
        + tap_weights[2] * padded[:, 2:]
    ).astype(jnp.bfloat16)
    first_mixed = apply_mix(block_mixes[0], conv_out).astype(jnp.bfloat16)
    first_peer = partner(first_mixed, far_bit)
    second_mixed = (
        apply_mix(block_mixes[1], first_mixed) + apply_mix(block_mixes[2], first_peer)
    ).astype(jnp.bfloat16)
    third_mixed = apply_mix(block_mixes[3], second_mixed).astype(jnp.bfloat16)
    third_peer = partner(third_mixed, near_bit)
    fourth_mixed = apply_mix(block_mixes[4], third_mixed) + apply_mix(block_mixes[5], third_peer)
    token_values = tokens.astype(jnp.float32)
    gate_in = gate_gain * token_values
    gate_sigmoid = jax.nn.sigmoid(gate_in)
    upstream = cotangent.astype(jnp.float32)
    grad_fourth = (upstream * gate_in * gate_sigmoid).astype(jnp.bfloat16)
    grad_gate = upstream * fourth_mixed * gate_sigmoid * (1.0 + gate_in * (1.0 - gate_sigmoid))
    gain_part = tok_scale * jnp.sum(grad_gate * token_values, axis=(0, 1))
    fourth_peer = partner(grad_fourth, near_bit)
    grad_third = (
        apply_transposed(block_mixes[4], grad_fourth)
        + apply_transposed(block_mixes[5], fourth_peer)
    ).astype(jnp.bfloat16)
    upper_peer = outer_sum(grad_fourth, third_peer)
    grad_second = apply_transposed(block_mixes[3], grad_third).astype(jnp.bfloat16)
    upper_grads = (
        jnp.stack(
            [outer_sum(grad_third, second_mixed), outer_sum(grad_fourth, third_mixed), upper_peer]
        )
        * mix_scale
    )
    second_peer = partner(grad_second, far_bit)
    grad_first = (
        apply_transposed(block_mixes[1], grad_second)
        + apply_transposed(block_mixes[2], second_peer)
    ).astype(jnp.bfloat16)
    lower_peer = outer_sum(grad_second, first_peer)
    grad_conv = apply_transposed(block_mixes[0], grad_first).astype(jnp.bfloat16)
    lower_grads = (
        jnp.stack(
            [outer_sum(grad_first, conv_out), outer_sum(grad_second, first_mixed), lower_peer]
        )
        * mix_scale
    )
    grad_values = grad_conv.astype(jnp.float32)
    padded_values = padded.astype(jnp.float32)
    taps_part = tok_scale * jnp.stack(
        [
            jnp.sum(grad_values * padded_values[:, :-2], axis=(0, 1)),
            jnp.sum(grad_values * padded_values[:, 1:-1], axis=(0, 1)),
            jnp.sum(grad_values * padded_values[:, 2:], axis=(0, 1)),
        ]
    )
    grad_padded = extend(grad_conv).astype(jnp.float32)
    input_grad = (
        tap_weights[0] * grad_padded[:, 2:]
        + tap_weights[1] * grad_padded[:, 1:-1]
        + tap_weights[2] * grad_padded[:, :-2]
        + grad_gate * gate_gain
    ).astype(jnp.bfloat16)
    local_grads = jnp.concatenate([lower_grads, upper_grads], axis=0)
    mixes_grad, taps_grad, gain_grad = lax.psum((local_grads, taps_part, gain_part), ("dp", "seq"))
    return (input_grad, mixes_grad, taps_grad, gain_grad)


def solution(mesh):
    placed = (P("dp", "seq", None), P("dp", "seq", None), P(), P(), P())
    return jax.shard_map(
        local,
        mesh=mesh,
        in_specs=placed,
        out_specs=(P("dp", "seq", None), P(), P(), P()),
        check_vma=False,
    )
```

profile of v0, /device:TPU:1, one launch (start us, length us, event | category | flops | bytes accessed | tf_op | source)
XLA Modules:
  0.0 396.5 jit_solution(5335751916178747653)
XLA Ops:
  7.2 0.8 fusion.78
  8.1 4.0 %collective-permute-start.4 = (bf16[1,1,1536]{2,1,0:T(2,128)(2,1)S(1)}, bf16[1,1,1536]{2,1,0:T(2,128)(2,1)S(1)}, u32[]{:S(2)}, u32[]{:S(2)}) collective-permute-start(bf16[1,1,1536]{2,1,0:T(2,128)(2,1)S(1)} %get-tuple-element.14), channel_id=1, source_target_pairs={{0,1},{1,2},{2,3},{3,4},{4,5},{5,6},{6,7},{7,8},{8,9},{9,10},{10,1... | collective-permute-start | bytes 9224 | tf_op jit(solution)/shard_map/ppermute | solution.py:17
  12.1 1.3 collective-permute-start.5
  13.4 1.9 fusion.15
  15.3 4.1 %collective-permute-start = (bf16[1,256,1536]{2,1,0:T(8,128)(2,1)S(1)}, bf16[1,256,1536]{2,1,0:T(8,128)(2,1)S(1)}, u32[]{:S(2)}, u32[]{:S(2)}) collective-permute-start(bf16[1,256,1536]{2,1,0:T(8,128)(2,1)S(1)} %fusion.15), channel_id=1, source_target_pairs={{0,1},{1,0},{2,3},{3,2},{4,5},{5,4},{6,7},{7,6},{8,9},{9,8},{10,11... | collective-permute-start | bytes 2359304 | tf_op jit(solution)/shard_map/ppermute | solution.py:27
  19.4 0.4 fusion.50
  20.0 0.8 convolution_convert_fusion.1
  20.8 6.6 %collective-permute-start.6 = (bf16[1,256,1536]{1,2,0:T(8,128)(2,1)S(1)}, bf16[1,256,1536]{1,2,0:T(8,128)(2,1)S(1)}, u32[]{:S(2)}, u32[]{:S(2)}) collective-permute-start(bf16[1,256,1536]{1,2,0:T(8,128)(2,1)S(1)} %bitcast.144), channel_id=1, source_target_pairs={{0,16},{1,17},{2,18},{3,19},{4,20},{5,21},{6,22},{7,23},{8,24},{9,... | collective-permute-start | bytes 2359304 | tf_op jit(solution)/shard_map/ppermute | solution.py:27
  28.1 4.9 %collective-permute-done = bf16[1,256,1536]{2,1,0:T(8,128)(2,1)S(1)} collective-permute-done((bf16[1,256,1536]{2,1,0:T(8,128)(2,1)S(1)}, bf16[1,256,1536]{2,1,0:T(8,128)(2,1)S(1)}, u32[]{:S(2)}, u32[]{:S(2)}) %collective-permute-start) | collective-permute-done | bytes 786464 | tf_op jit(solution)/shard_map/ppermute | solution.py:27
  33.0 0.4 fusion.10
  33.8 10.9 %collective-permute-start.1 = (bf16[1,256,1536]{1,2,0:T(8,128)(2,1)S(1)}, bf16[1,256,1536]{1,2,0:T(8,128)(2,1)S(1)}, u32[]{:S(2)}, u32[]{:S(2)}) collective-permute-start(bf16[1,256,1536]{1,2,0:T(8,128)(2,1)S(1)} %bitcast.143), channel_id=1, source_target_pairs={{0,16},{1,17},{2,18},{3,19},{4,20},{5,21},{6,22},{7,23},{8,24},{9,... | collective-permute-start | bytes 2359304 | tf_op jit(solution)/shard_map/ppermute | solution.py:27
  45.4 31.9 %collective-permute-done.6 = bf16[1,256,1536]{1,2,0:T(8,128)(2,1)S(1)} collective-permute-done((bf16[1,256,1536]{1,2,0:T(8,128)(2,1)S(1)}, bf16[1,256,1536]{1,2,0:T(8,128)(2,1)S(1)}, u32[]{:S(2)}, u32[]{:S(2)}) %collective-permute-start.6) | collective-permute-done | bytes 786464 | tf_op jit(solution)/shard_map/ppermute | solution.py:27
  78.4 3.6 collective-permute-start.7
  83.3 10.9 %collective-permute-done.1 = bf16[1,256,1536]{1,2,0:T(8,128)(2,1)S(1)} collective-permute-done((bf16[1,256,1536]{1,2,0:T(8,128)(2,1)S(1)}, bf16[1,256,1536]{1,2,0:T(8,128)(2,1)S(1)}, u32[]{:S(2)}, u32[]{:S(2)}) %collective-permute-start.1) | collective-permute-done | bytes 786464 | tf_op jit(solution)/shard_map/ppermute | solution.py:27
  94.5 0.8 fusion.24
  95.4 3.6 collective-permute-start.2
  98.9 1.3 collective-permute-start.3
  100.2 0.8 convolution_bitcast_fusion.5
  102.1 1.2 pad_maximum_fusion
  103.5 1.4 maximum_convert_fusion
  105.0 2.5 fusion.23
  107.6 106.9 %all-reduce = (f32[3,1536]{1,0:T(4,128)}, f32[1536]{0:T(1024)}) all-reduce(f32[3,1536]{1,0:T(4,128)S(1)} %maximum_multiply_fusion.2, f32[1536]{0:T(1024)S(1)} %broadcast_multiply_fusion), channel_id=1, replica_groups=mesh['dp'=16,'seq'=32] {'dp','seq'}, use_global_device_ids=true, to_apply=%region_4.0 | all-reduce | flops 6144 | bytes 49152 | tf_op jit(solution)/shard_map/psum | solution.py:124
  214.5 172.5 %all-reduce.3.cloned.1.call-done = f32[6,256,256]{2,1,0:T(8,128)} async-done(((f32[6,256,256]{2,1,0:T(8,128)}), f32[6,256,256]{2,1,0:T(8,128)}) %all-reduce.3.cloned.1.call-update) | async-done | bytes 1572880 | tf_op jit(solution)/shard_map/psum | solution.py:124
  386.9 2.7 copy.10
  (46 shorter events, 5.8 us)
Async XLA Ops:
  7.2 12.2 %copy-start.6 = (bf16[3,1536]{1,0:T(4,128)(2,1)S(1)}, bf16[3,1536]{1,0:T(4,128)(2,1)}, u32[]{:S(2)}) copy-start(bf16[3,1536]{1,0:T(4,128)(2,1)} %param.7) | copy-start | bytes 27652
  7.2 12.3 %copy-start.1 = (bf16[6,256,256]{2,1,0:T(8,128)(2,1)S(1)}, bf16[6,256,256]{2,1,0:T(8,128)(2,1)}, u32[]{:S(2)}) copy-start(bf16[6,256,256]{2,1,0:T(8,128)(2,1)} %param.8) | copy-start | bytes 2359300
  7.2 379.8 %all-reduce.3.cloned.1.call-start = ((), (), s32[]{:S(2)}) async-start(), calls=%async_computation | async-start | bytes 3145728 | tf_op jit(solution)/shard_map/psum | solution.py:124
  8.1 11.9 %collective-permute-start.4 = (bf16[1,1,1536]{2,1,0:T(2,128)(2,1)S(1)}, bf16[1,1,1536]{2,1,0:T(2,128)(2,1)S(1)}, u32[]{:S(2)}, u32[]{:S(2)}) collective-permute-start(bf16[1,1,1536]{2,1,0:T(2,128)(2,1)S(1)} %get-tuple-element.14), channel_id=1, source_target_pairs={{0,1},{1,2},{2,3},{3,4},{4,5},{5,6},{6,7},{7,8},{8,9},{9,10},{10,1... | collective-permute-start | bytes 9224 | tf_op jit(solution)/shard_map/ppermute | solution.py:17
  12.1 7.8 %collective-permute-start.5 = (bf16[1,1,1536]{2,1,0:T(2,128)(2,1)S(1)}, bf16[1,1,1536]{2,1,0:T(2,128)(2,1)S(1)}, u32[]{:S(2)}, u32[]{:S(2)}) collective-permute-start(bf16[1,1,1536]{2,1,0:T(2,128)(2,1)S(1)} %get-tuple-element.15), channel_id=1, source_target_pairs={{1,0},{2,1},{3,2},{4,3},{5,4},{6,5},{7,6},{8,7},{9,8},{10,9},{11,1... | collective-permute-start | bytes 9224 | tf_op jit(solution)/shard_map/ppermute | solution.py:19
  15.3 4.7 %copy-start = (bf16[1,256,1536]{2,1,0:T(8,128)(2,1)S(1)}, bf16[1,256,1536]{2,1,0:T(8,128)(2,1)}, u32[]{:S(2)}) copy-start(bf16[1,256,1536]{2,1,0:T(8,128)(2,1)} %param.5) | copy-start | bytes 2359300
  15.3 17.7 %collective-permute-start = (bf16[1,256,1536]{2,1,0:T(8,128)(2,1)S(1)}, bf16[1,256,1536]{2,1,0:T(8,128)(2,1)S(1)}, u32[]{:S(2)}, u32[]{:S(2)}) collective-permute-start(bf16[1,256,1536]{2,1,0:T(8,128)(2,1)S(1)} %fusion.15), channel_id=1, source_target_pairs={{0,1},{1,0},{2,3},{3,2},{4,5},{5,4},{6,7},{7,6},{8,9},{9,8},{10,11... | collective-permute-start | bytes 2359304 | tf_op jit(solution)/shard_map/ppermute | solution.py:27
  20.8 56.5 %collective-permute-start.6 = (bf16[1,256,1536]{1,2,0:T(8,128)(2,1)S(1)}, bf16[1,256,1536]{1,2,0:T(8,128)(2,1)S(1)}, u32[]{:S(2)}, u32[]{:S(2)}) collective-permute-start(bf16[1,256,1536]{1,2,0:T(8,128)(2,1)S(1)} %bitcast.144), channel_id=1, source_target_pairs={{0,16},{1,17},{2,18},{3,19},{4,20},{5,21},{6,22},{7,23},{8,24},{9,... | collective-permute-start | bytes 2359304 | tf_op jit(solution)/shard_map/ppermute | solution.py:27
  33.8 60.4 %collective-permute-start.1 = (bf16[1,256,1536]{1,2,0:T(8,128)(2,1)S(1)}, bf16[1,256,1536]{1,2,0:T(8,128)(2,1)S(1)}, u32[]{:S(2)}, u32[]{:S(2)}) collective-permute-start(bf16[1,256,1536]{1,2,0:T(8,128)(2,1)S(1)} %bitcast.143), channel_id=1, source_target_pairs={{0,16},{1,17},{2,18},{3,19},{4,20},{5,21},{6,22},{7,23},{8,24},{9,... | collective-permute-start | bytes 2359304 | tf_op jit(solution)/shard_map/ppermute | solution.py:27
  78.4 22.7 %collective-permute-start.7 = (bf16[1,256,1536]{1,2,0:T(8,128)(2,1)S(1)}, bf16[1,256,1536]{1,2,0:T(8,128)(2,1)S(1)}, u32[]{:S(2)}, u32[]{:S(2)}) collective-permute-start(bf16[1,256,1536]{1,2,0:T(8,128)(2,1)S(1)} %bitcast.142), channel_id=1, source_target_pairs={{0,1},{1,0},{2,3},{3,2},{4,5},{5,4},{6,7},{7,6},{8,9},{9,8},{10,11... | collective-permute-start | bytes 2359304 | tf_op jit(solution)/shard_map/ppermute | solution.py:27
  95.3 6.4 %copy-start.2 = (bf16[1,256,1536]{2,1,0:T(8,128)(2,1)}, bf16[1,256,1536]{2,1,0:T(8,128)(2,1)S(1)}, u32[]{:S(2)}) copy-start(bf16[1,256,1536]{2,1,0:T(8,128)(2,1)S(1)} %get-tuple-element.18) | copy-start | bytes 2359300
  95.4 8.0 %collective-permute-start.2 = (bf16[1,1,1536]{2,1,0:T(2,128)(2,1)S(1)}, bf16[1,1,1536]{2,1,0:T(2,128)(2,1)S(1)}, u32[]{:S(2)}, u32[]{:S(2)}) collective-permute-start(bf16[1,1,1536]{2,1,0:T(2,128)(2,1)S(1)} %get-tuple-element.16), channel_id=1, source_target_pairs={{0,1},{1,2},{2,3},{3,4},{4,5},{5,6},{6,7},{7,8},{8,9},{9,10},{10,1... | collective-permute-start | bytes 9224 | tf_op jit(solution)/shard_map/ppermute | solution.py:17
  98.9 4.6 %collective-permute-start.3 = (bf16[1,1,1536]{2,1,0:T(2,128)(2,1)S(1)}, bf16[1,1,1536]{2,1,0:T(2,128)(2,1)S(1)}, u32[]{:S(2)}, u32[]{:S(2)}) collective-permute-start(bf16[1,1,1536]{2,1,0:T(2,128)(2,1)S(1)} %get-tuple-element.17), channel_id=1, source_target_pairs={{1,0},{2,1},{3,2},{4,3},{5,4},{6,5},{7,6},{8,7},{9,8},{10,9},{11,1... | collective-permute-start | bytes 9224 | tf_op jit(solution)/shard_map/ppermute | solution.py:19
  101.2 0.9 copy-start.3
  103.3 1.6 copy-start.4
  103.4 1.6 copy-start.5
  103.4 1.6 copy-start.7
Sparse Core Ops, SparseCore 0:
  103.5 283.4 all-reduce.2
where the time goes:
time: 397 us
  waiting for transfers between devices  220 us (55%)
  blocking collectives  107 us (27%)
  starting transfers between devices  35.4 us (9%)
  between operations  14.4 us (4%)
  matrix products  10.5 us (3%)
  other arithmetic  4.95 us (1%)
  local copies, waits for them, and re-layouts  4.11 us (1%)
    psum x1, waiting for transfers between devices, local(): lax.psum((local_grads, taps_part, gain_part), ('dp', 'seq'))  172 us
    psum x1, blocking collectives, local(): lax.psum((local_grads, taps_part, gain_part), ('dp', 'seq'))  107 us
    ppermute x4, waiting for transfers between devices, partner_2(): lax.ppermute(shard, axis, [(i, i ^ 1 << distance) for i in range(lax.axis...  47.6 us
    ppermute x4, starting transfers between devices, partner_2(): lax.ppermute(shard, axis, [(i, i ^ 1 << distance) for i in range(lax.axis...  25.2 us
  transfers between devices with their start and end apart: 9, of which 5 were waited for; matrix products, arithmetic and copies ran while one was open for 4% of the time, Pallas kernels for 0%

commit v1 on v0

v1 whole, which is shorter than its diff:
```python
import functools
import math

import jax
import jax.numpy as jnp
from jax import lax
from jax.experimental import pallas as pl
from jax.experimental.pallas import tpu as pltpu
from jax.sharding import PartitionSpec as P

F32, BF16 = jnp.float32, jnp.bfloat16
MESH = pl.DeviceIdType.MESH

CORES, XS, YS, ZLO, ZHI = 2, 4, 8, 4, 2
ZS = ZLO * ZHI
T, D = 256, 1536
QUARTER = D // 4
LANES = 128
CHUNKS = QUARTER // LANES
WIDE = 4 * LANES
EDGE = 16
TILE = 16
ROWS = 6 * T * T // LANES
HALF, PX, PY = ROWS // CORES, ROWS // (CORES * XS), ROWS // (CORES * XS * YS)


def far(v):
    return jnp.concatenate([v[:, 2 * LANES :], v[:, : 2 * LANES]], axis=1)


def near(v):
    a, b, c, d = (v[:, i * LANES : (i + 1) * LANES] for i in range(4))
    return jnp.concatenate([b, a, d, c], axis=1)


def mm(a, b):
    return jnp.dot(a, b, preferred_element_type=F32)


def mm_nt(a, b):
    return lax.dot_general(a, b, (((1,), (1,)), ((), ())), preferred_element_type=F32)


def kernel(
    tok_hbm, cot_hbm, taps_ref, mixes_ref, gain_ref,
    out_hbm, ag, e_out,
    tok, cot, halo, pad, conv, gf2, h, f2, t2, s2, gt, gs2, g1, fourth,
    gcpad, ggg, outb, edge_out, edges, wts,
    m0, m12, m3, m45, m0t, m12t, m3t, m45t,
    grads, own_x, own_y, core_out, core_in, x_out, x_in, y_out, y_in, z_in,
    e_own, e_core, e_x, e_y, e_z,
    in_send, in_recv, in_local, halo_send, halo_recv, edge_send, edge_recv,
    out_send, out_recv, out_local, core_sem, x_send, x_recv, y_send, y_recv,
    z_send, z_recv, gy_send, gy_recv, gx_send, gx_recv, gc_send, gc_recv,
    ec_sem, ex_send, ex_recv, ey_send, ey_recv, ez_send, ez_recv, eq_send, eq_recv,
):
    dp, k = lax.axis_index("dp"), lax.axis_index("seq")
    core, x, z_hi = lax.rem(dp, CORES), lax.rem(lax.div(dp, CORES), XS), lax.div(dp, CORES * XS)
    y, z_lo = lax.rem(k, YS), lax.div(k, YS)
    z = z_hi * ZLO + z_lo
    yb, yp = lax.rem(y, 2), lax.div(y, 2)
    zb, zp = lax.div(z_lo, 2), lax.rem(z_lo, 2)
    q = yb + 2 * zb

    def at(core_=core, x_=x, y_=y, z_=z):
        return (lax.div(z_, ZLO) * (XS * CORES) + x_ * CORES + core_, lax.rem(z_, ZLO) * YS + y_)

    def in_group(yp_, zp_, quarter):
        return (dp, (zp_ + 2 * lax.div(quarter, 2)) * YS + 2 * yp_ + lax.rem(quarter, 2))

    last_y, first_y = yp == YS // 2 - 1, yp == 0
    next_yp, next_zp = lax.rem(yp + 1, YS // 2), jnp.where(last_y, 1 - zp, zp)
    prev_yp, prev_zp = lax.rem(yp + YS // 2 - 1, YS // 2), jnp.where(first_y, 1 - zp, zp)
    next_flip = jnp.where(last_y, zp, 0)
    prev_flip = jnp.where(first_y, 1 - zp, 0)
    has_prev = 1.0 - prev_flip.astype(F32)
    has_next = 1.0 - next_flip.astype(F32)

    mates = [lax.rem(q + m, 4) for m in range(1, 4)]

    def rcopy(src, dst, send, recv, device):
        return pltpu.make_async_remote_copy(
            src_ref=src, dst_ref=dst, send_sem=send, recv_sem=recv, device_id=device, device_id_type=MESH
        )

    def lanes(quarter, c):
        return pl.ds(pl.multiple_of(quarter * QUARTER + c * LANES, LANES), LANES)

    barrier = pltpu.get_barrier_semaphore()
    others = [in_group(yp, zp, m) for m in mates]
    others += [in_group(next_yp, next_zp, m) for m in range(4)]
    others += [in_group(prev_yp, prev_zp, m) for m in range(4)]
    others += [at(core_=1 - core)]
    others += [at(x_=lax.rem(x + i, XS)) for i in range(1, XS)]
    others += [at(y_=lax.rem(y + i, YS)) for i in range(1, YS)]
    others += [at(z_=lax.rem(z + i, ZS)) for i in range(1, ZS)]
    for device in others:
        pl.semaphore_signal(barrier, inc=1, device_id=device, device_id_type=MESH)
    pl.semaphore_wait(barrier, len(others))

    halo_yp, halo_zp = jnp.where(yb == 1, next_yp, prev_yp), jnp.where(yb == 1, next_zp, prev_zp)
    halo_flip = jnp.where(yb == 1, next_flip, prev_flip)
    halo_half = lax.rem(zb + halo_flip, 2)
    halo_slot = (1 - yb) * 2 + halo_half
    halo_row = pl.multiple_of(yb * (T - EDGE), EDGE)
    halo_copies = [
        rcopy(
            tok_hbm.at[pl.ds(halo_row, EDGE), pl.ds(m * QUARTER, QUARTER)],
            halo.at[halo_slot],
            halo_send.at[m],
            halo_recv.at[halo_slot],
            in_group(halo_yp, halo_zp, m),
        )
        for m in range(4)
    ]
    for copy in halo_copies:
        copy.start()

    def inbound(c, arrays=(0, 1)):
        copies = []
        for m in (1, 2, 0):
            for a in arrays:
                src, dst = ((tok_hbm, tok), (cot_hbm, cot))[a]
                copies.append(
                    rcopy(
                        src.at[:, lanes(mates[m], c)],
                        dst.at[c, q],
                        in_send.at[a, c, m],
                        in_recv.at[a, c, 2 - m],
                        in_group(yp, zp, mates[m]),
                    )
                )
        return copies

    def local(c):
        return [
            pltpu.make_async_copy(src.at[:, lanes(q, c)], dst.at[c, q], in_local.at[a, c])
            for a, (src, dst) in enumerate(((tok_hbm, tok), (cot_hbm, cot)))
        ]

    for c in range(CHUNKS):
        for copy in inbound(c) + local(c):
            copy.start()

    def transposed(v):
        return v.astype(F32).T.astype(BF16)

    m0[...] = mixes_ref[0]
    m12[:, :T], m12[:, T:] = mixes_ref[1], mixes_ref[2]
    m3[...] = mixes_ref[3]
    m45[:, :T], m45[:, T:] = mixes_ref[4], mixes_ref[5]
    m0t[...] = transposed(mixes_ref[0])
    m12t[:, :T], m12t[:, T:] = transposed(mixes_ref[1]), transposed(mixes_ref[2])
    m3t[...] = transposed(mixes_ref[3])
    m45t[:, :T], m45t[:, T:] = transposed(mixes_ref[4]), transposed(mixes_ref[5])
    wts[0:3, :] = taps_ref[...].astype(F32)
    wts[3:4, :] = gain_ref[...]
    grads[...] = jnp.zeros_like(grads)
    e_own[...] = jnp.zeros_like(e_own)

    def weights(c):
        w = wts[:, lanes(q, c)]
        w = jnp.concatenate([w] * 4, axis=1)
        return [w[i : i + 1] for i in range(4)]

    def fill_edges(ref, prev, nxt):
        body = ref[8 : 16, :], ref[T : T + 8, :]
        first, last = body[0][0:1], body[1][7:8]
        ref[7:8, :] = jnp.concatenate([prev[0], last[:, :LANES], prev[1], last[:, 2 * LANES : 3 * LANES]], axis=1)
        ref[T + 8 : T + 9, :] = jnp.concatenate(
            [first[:, LANES : 2 * LANES], nxt[0], first[:, 3 * LANES :], nxt[1]], axis=1
        )

    def mask_edges(prev, nxt):
        return [prev[0] * has_prev, prev[1]], [nxt[0], nxt[1] * has_next]

    def tile_rows(i):
        return pl.ds(pl.multiple_of(i * TILE, TILE), TILE)

    def window(ref, i):
        w = ref[pl.ds(pl.multiple_of(i * TILE, TILE), TILE + 16), :]
        return w[7 : 7 + TILE], w[8 : 8 + TILE], w[9 : 9 + TILE]

    def edge_copies(c):
        copies = []
        for half in range(2):
            for side, (yp_, zp_, flip) in enumerate(((next_yp, next_zp, next_flip), (prev_yp, prev_zp, prev_flip))):
                slot = side * 2 + lax.rem(half + flip, 2)
                copies.append(
                    rcopy(
                        edge_out.at[c, side * 2 + half],
                        edges.at[c, slot],
                        edge_send.at[c, side * 2 + half],
                        edge_recv.at[c, slot],
                        in_group(yp_, zp_, q),
                    )
                )
        return copies

    def edge_wait(c):
        for slot in range(4):
            rcopy(
                edge_out.at[c, slot], edges.at[c, slot], edge_send.at[c, slot], edge_recv.at[c, slot],
                in_group(next_yp, next_zp, q),
            ).wait_recv()

    def wait_inbound(c):
        for a in range(2):
            dst = (tok, cot)[a]
            for m in range(3):
                rcopy(
                    dst.at[c, q], dst.at[c, mates[m]], in_send.at[a, c, m], in_recv.at[a, c, m],
                    in_group(yp, zp, mates[m]),
                ).wait_recv()
        for copy in local(c):
            copy.wait()

    def chain(c):
        for b in range(4):
            pad[8 : 8 + T, b * LANES : (b + 1) * LANES] = tok[c, b].astype(F32)
        chunk = pl.ds(pl.multiple_of(c * LANES, LANES), LANES)
        ends = [halo[s, :, chunk].astype(F32) for s in range(4)]
        fill_edges(
            pad, *mask_edges([ends[0][EDGE - 1 :], ends[1][EDGE - 1 :]], [ends[2][:1], ends[3][:1]])
        )
        w = weights(c)

        def before(i, carry):
            prev, cur, nxt = window(pad, i)
            rows = tile_rows(i)
            conv[rows, :] = (w[0] * prev + w[1] * cur + w[2] * nxt).astype(BF16)
            up = jnp.concatenate([cot[c, b, rows, :] for b in range(4)], axis=1).astype(F32)
            gate = w[3] * cur
            sig = 1.0 / (1.0 + jnp.exp(-gate))
            gf = (up * gate * sig).astype(BF16)
            gf2[rows, :] = gf
            gf2[pl.ds(pl.multiple_of(T + i * TILE, TILE), TILE), :] = near(gf)
            h[rows, :] = up * sig * (1.0 + gate * (1.0 - sig))
            return carry

        lax.fori_loop(0, T // TILE, before, 0)

        first = mm(m0[...], conv[...]).astype(BF16)
        f2[:T, :], f2[T:, :] = first, far(first)
        third_grad = mm(m45t[...], gf2[...]).astype(BF16)
        gt[...] = third_grad
        s2[...] = mm(m12[...], f2[...]).astype(BF16)
        second_grad = mm(m3t[...], gt[...]).astype(BF16)
        gs2[:T, :], gs2[T:, :] = second_grad, far(second_grad)
        third = mm(m3[...], s2[...]).astype(BF16)
        t2[:T, :], t2[T:, :] = third, near(third)
        g1[...] = mm(m12t[...], gs2[...]).astype(BF16)
        fourth[...] = mm(m45[...], t2[...])
        gc = mm(m0t[...], g1[...]).astype(BF16)
        gcpad[c, 8 : 8 + T, :] = gc.astype(F32)
        for half in range(2):
            odd = slice((2 * half + 1) * LANES, (2 * half + 2) * LANES)
            even = slice(2 * half * LANES, (2 * half + 1) * LANES)
            edge_out[c, half] = gc[T - EDGE :, odd]
            edge_out[c, 2 + half] = gc[:EDGE, even]
        for copy in edge_copies(c):
            copy.start()

        def add_grad(i, value):
            grads[2 * i * T : (2 * i + 1) * T, :] += value[:, :LANES]
            grads[(2 * i + 1) * T : (2 * i + 2) * T, :] += value[:, LANES:]

        add_grad(0, mm_nt(g1[...], conv[...]))
        add_grad(3, mm_nt(gt[...], s2[...]))
        both = mm_nt(gs2[:T, :], f2[...])
        add_grad(1, both[:, :T])
        add_grad(2, both[:, T:])
        both = mm_nt(gf2[:T, :], t2[...])
        add_grad(4, both[:, :T])
        add_grad(5, both[:, T:])

    def sums(c):
        w = weights(c)

        def after(i, carry):
            prev, cur, nxt = window(pad, i)
            rows = tile_rows(i)
            gg = h[rows, :] * fourth[rows, :]
            gc = gcpad[c, pl.ds(pl.multiple_of(8 + i * TILE, 8), TILE), :]
            ggg[c, rows, :] = gg * w[3]

            def fold(v):
                return v[:8] + v[8:]

            return tuple(
                have + fold(v) for have, v in zip(carry, (gc * prev, gc * cur, gc * nxt, gg * cur))
            )

        zero = jnp.zeros((8, WIDE), F32)
        totals = lax.fori_loop(0, T // TILE, after, (zero,) * 4)
        for j, total in enumerate(totals):
            row = jnp.sum(total, axis=0, keepdims=True)
            e_own[c, j : j + 1, :] = sum(row[:, b * LANES : (b + 1) * LANES] for b in range(4))

    def finish(c):
        edge_wait(c)
        ends = [edges[c, s].astype(F32) for s in range(4)]
        fill_edges(
            gcpad.at[c], *mask_edges([ends[0][EDGE - 1 :], ends[1][EDGE - 1 :]], [ends[2][:1], ends[3][:1]])
        )
        w = weights(c)

        def close(i, carry):
            prev, cur, nxt = window(gcpad.at[c], i)
            rows = tile_rows(i)
            out = (w[0] * nxt + w[1] * cur + w[2] * prev + ggg[c, rows, :]).astype(BF16)
            for b in range(4):
                outb[c, b, rows, :] = out[:, b * LANES : (b + 1) * LANES]
            return carry

        lax.fori_loop(0, T // TILE, close, 0)

    def outbound(c):
        return [
            rcopy(
                outb.at[c, mates[m]],
                out_hbm.at[:, lanes(q, c)],
                out_send.at[c, m],
                out_recv.at[c, 2 - m],
                in_group(yp, zp, mates[m]),
            )
            for m in (1, 2, 0)
        ]

    def out_own(c):
        return pltpu.make_async_copy(outb.at[c, q], out_hbm.at[:, lanes(q, c)], out_local.at[c])

    def send_out(c):
        for copy in outbound(c):
            copy.start()
        out_own(c).start()

    for slot in range(4):
        rcopy(
            tok_hbm.at[pl.ds(0, EDGE), pl.ds(0, QUARTER)], halo.at[slot], halo_send.at[slot], halo_recv.at[slot],
            in_group(next_yp, next_zp, q),
        ).wait_recv()

    def step(c, carry):
        @pl.when(c > 0)
        def _():
            sums(c - 1)
            finish(c - 1)

        wait_inbound(c)

        @pl.when(c == CHUNKS - 1)
        def _():
            for past in range(CHUNKS - 1):
                send_out(past)

        chain(c)
        return carry

    lax.fori_loop(0, CHUNKS, step, 0)

    sibling = at(core_=1 - core)
    x_mates = [lax.rem(x + i, XS) for i in range(1, XS)]
    y_mates = [lax.rem(y + i, YS) for i in range(1, YS)]
    z_mates = [lax.rem(z + i, ZS) for i in range(1, ZS)]

    def rows_of(start, size):
        return pl.ds(pl.multiple_of(start, EDGE), size)

    core_out[...] = grads[rows_of((1 - core) * HALF, HALF), :].astype(BF16)
    core_copy = rcopy(core_out, core_in, core_sem.at[0], core_sem.at[1], sibling)
    core_copy.start()
    sums(CHUNKS - 1)
    e_core_copy = rcopy(e_own, e_core, ec_sem.at[0], ec_sem.at[1], sibling)
    e_core_copy.start()
    core_copy.wait_recv()
    x_copies = []
    for i, other in enumerate(x_mates):
        part = grads[rows_of(core * HALF + other * PX, PX), :] + core_in[rows_of(other * PX, PX), :].astype(F32)
        x_out[i] = part.astype(BF16)
        x_copies.append(rcopy(x_out.at[i], x_in.at[i], x_send.at[i], x_recv.at[i], at(x_=other)))
        x_copies[-1].start()
    own_x[...] = grads[rows_of(core * HALF + x * PX, PX), :] + core_in[rows_of(x * PX, PX), :].astype(F32)

    e_core_copy.wait_recv()
    e_x[x] = e_own[...] + e_core[...]
    ex_copies = [
        rcopy(e_x.at[x], e_x.at[x], ex_send.at[i], ex_recv.at[i], at(x_=other)) for i, other in enumerate(x_mates)
    ]
    for copy in ex_copies:
        copy.start()

    finish(CHUNKS - 1)
    send_out(CHUNKS - 1)

    for copy in x_copies:
        copy.wait_recv()
    own_x[...] += x_in[0].astype(F32) + x_in[1].astype(F32) + x_in[2].astype(F32)
    y_out[...] = own_x[...].astype(BF16)
    y_copies = [
        rcopy(y_out.at[rows_of(other * PY, PY)], y_in.at[i], y_send.at[i], y_recv.at[i], at(y_=other))
        for i, other in enumerate(y_mates)
    ]
    for copy in y_copies:
        copy.start()

    def slot_wait(ref, slot, send, recv, device):
        rcopy(ref.at[slot], ref.at[slot], send, recv, device).wait_recv()

    for i in range(XS - 1):
        slot_wait(e_x, lax.rem(x + XS - 1 - i, XS), ex_send.at[i], ex_recv.at[i], sibling)
    e_y[yp] = e_x[0] + e_x[1] + e_x[2] + e_x[3]
    ey_copies = [
        rcopy(e_y.at[yp], e_y.at[yp], ey_send.at[i], ey_recv.at[i], at(y_=lax.rem(y + 2 * (i + 1), YS)))
        for i in range(3)
    ]
    for copy in ey_copies:
        copy.start()

    for copy in y_copies:
        copy.wait_recv()
    total = own_x[rows_of(y * PY, PY), :]
    for i in range(YS - 1):
        total = total + y_in[i].astype(F32)
    z_in[z] = total.astype(BF16)
    z_copies = [
        rcopy(z_in.at[z], z_in.at[z], z_send.at[i], z_recv.at[i], at(z_=other)) for i, other in enumerate(z_mates)
    ]
    for copy in z_copies:
        copy.start()

    for i in range(3):
        slot_wait(e_y, lax.rem(yp + 3 - i, 4), ey_send.at[i], ey_recv.at[i], sibling)
    ez_me = z_hi * 2 + zp
    e_z[ez_me] = e_y[0] + e_y[1] + e_y[2] + e_y[3]

    def ez_device(slot):
        return at(z_=lax.div(slot, 2) * ZLO + 2 * zb + lax.rem(slot, 2))

    ez_copies = [
        rcopy(e_z.at[ez_me], e_z.at[ez_me], ez_send.at[i], ez_recv.at[i], ez_device(lax.rem(ez_me + i + 1, 4)))
        for i in range(3)
    ]
    for copy in ez_copies:
        copy.start()

    for i in range(ZS - 1):
        slot_wait(z_in, lax.rem(z + ZS - 1 - i, ZS), z_send.at[i], z_recv.at[i], sibling)
    total = z_in[0].astype(F32)
    for i in range(1, ZS):
        total = total + z_in[i].astype(F32)
    own = rows_of(core * HALF + x * PX + y * PY, PY)
    ag[own, :] = total.astype(BF16)
    gy_copies = [
        rcopy(ag.at[own], ag.at[own], gy_send.at[i], gy_recv.at[i], at(y_=other)) for i, other in enumerate(y_mates)
    ]
    for copy in gy_copies:
        copy.start()

    for i in range(3):
        slot_wait(e_z, lax.rem(ez_me + 3 - i, 4), ez_send.at[i], ez_recv.at[i], sibling)
    e_out[q] = e_z[0] + e_z[1] + e_z[2] + e_z[3]
    eq_copies = [
        rcopy(e_out.at[q], e_out.at[q], eq_send.at[i], eq_recv.at[i], in_group(yp, zp, mates[i])) for i in range(3)
    ]
    for copy in eq_copies:
        copy.start()

    for i in range(YS - 1):
        there = rows_of(core * HALF + x * PX + lax.rem(y + YS - 1 - i, YS) * PY, PY)
        rcopy(ag.at[there], ag.at[there], gy_send.at[i], gy_recv.at[i], sibling).wait_recv()
    mine = rows_of(core * HALF + x * PX, PX)
    gx_copies = [
        rcopy(ag.at[mine], ag.at[mine], gx_send.at[i], gx_recv.at[i], at(x_=other)) for i, other in enumerate(x_mates)
    ]
    for copy in gx_copies:
        copy.start()
    gc_copies = [rcopy(ag.at[mine], ag.at[mine], gc_send.at[0], gc_recv.at[0], sibling)]
    gc_copies[0].start()
    for i in range(XS - 1):
        there = rows_of(core * HALF + lax.rem(x + XS - 1 - i, XS) * PX, PX)
        rcopy(ag.at[there], ag.at[there], gx_send.at[i], gx_recv.at[i], sibling).wait_recv()
        gc_copies.append(rcopy(ag.at[there], ag.at[there], gc_send.at[i + 1], gc_recv.at[i + 1], sibling))
        gc_copies[-1].start()

    for i in range(3):
        slot_wait(e_out, mates[2 - i], eq_send.at[i], eq_recv.at[i], sibling)
    for c in range(CHUNKS):
        for m in range(3):
            rcopy(
                outb.at[c, mates[m]], out_hbm.at[:, lanes(mates[m], c)], out_send.at[c, m], out_recv.at[c, m], sibling
            ).wait_recv()
        out_own(c).wait()
    for i in range(XS):
        there = rows_of((1 - core) * HALF + lax.rem(x + XS - i, XS) * PX, PX)
        rcopy(ag.at[there], ag.at[there], gc_send.at[i], gc_recv.at[i], sibling).wait_recv()
    sent = halo_copies + [core_copy, e_core_copy] + x_copies + ex_copies + y_copies + ey_copies
    sent += z_copies + ez_copies + gy_copies + eq_copies + gx_copies + gc_copies
    for c in range(CHUNKS):
        sent += inbound(c) + edge_copies(c) + outbound(c)
    for copy in sent:
        copy.wait_send()


def local(tokens, cotangent, conv_taps, block_mixes, gate_gain):
    slabs = lax.axis_size("dp")
    tok_scale = 1.0 / math.sqrt(slabs * lax.axis_size("seq") * T)
    mix_scale = 1.0 / math.sqrt(slabs * lax.axis_size("seq") * D)
    small = (CHUNKS, 8, LANES)
    dma = pltpu.SemaphoreType.DMA
    wide = (T, WIDE)
    scratch = [
        *[pltpu.VMEM((CHUNKS, 4, T, LANES), BF16)] * 2,
        pltpu.VMEM((4, EDGE, QUARTER), BF16),
        pltpu.VMEM((T + 16, WIDE), F32),
        pltpu.VMEM(wide, BF16),
        pltpu.VMEM((2 * T, WIDE), BF16),
        pltpu.VMEM(wide, F32),
        pltpu.VMEM((2 * T, WIDE), BF16),
        pltpu.VMEM((2 * T, WIDE), BF16),
        pltpu.VMEM(wide, BF16),
        pltpu.VMEM(wide, BF16),
        pltpu.VMEM((2 * T, WIDE), BF16),
        pltpu.VMEM(wide, BF16),
        pltpu.VMEM(wide, F32),
        pltpu.VMEM((CHUNKS, T + 16, WIDE), F32),
        pltpu.VMEM((CHUNKS, T, WIDE), F32),
        pltpu.VMEM((CHUNKS, 4, T, LANES), BF16),
        *[pltpu.VMEM((CHUNKS, 4, EDGE, LANES), BF16)] * 2,
        pltpu.VMEM((8, D), F32),
        *[pltpu.VMEM((T, n * T), BF16) for n in (1, 2, 1, 2, 1, 2, 1, 2)],
        pltpu.VMEM((ROWS, LANES), F32),
        pltpu.VMEM((PX, LANES), F32),
        pltpu.VMEM((PY, LANES), F32),
        *[pltpu.VMEM((HALF, LANES), BF16)] * 2,
        *[pltpu.VMEM((XS - 1, PX, LANES), BF16)] * 2,
        pltpu.VMEM((PX, LANES), BF16),
        pltpu.VMEM((YS - 1, PY, LANES), BF16),
        pltpu.VMEM((ZS, PY, LANES), BF16),
        *[pltpu.VMEM(small, F32)] * 2,
        *[pltpu.VMEM((4, *small), F32)] * 3,
        *[dma((2, CHUNKS, 3))] * 2, dma((2, CHUNKS)),
        *[dma((4,))] * 2,
        *[dma((CHUNKS, 4))] * 2,
        *[dma((CHUNKS, 3))] * 2, dma((CHUNKS,)),
        dma((2,)),
        *[dma((XS - 1,))] * 2,
        *[dma((YS - 1,))] * 2,
        *[dma((ZS - 1,))] * 2,
        *[dma((YS - 1,))] * 2,
        *[dma((XS - 1,))] * 2,
        *[dma((XS,))] * 2,
        dma((2,)),
        *[dma((3,))] * 8,
    ]
    vmem, hbm = pl.BlockSpec(memory_space=pltpu.VMEM), pl.BlockSpec(memory_space=pl.ANY)
    flops = 18 * 2 * T * T * D
    input_grad, mixes, small_sums = pl.pallas_call(
        kernel,
        out_shape=(
            jax.ShapeDtypeStruct((T, D), BF16),
            jax.ShapeDtypeStruct((ROWS, LANES), BF16),
            jax.ShapeDtypeStruct((4, *small), F32),
        ),
        in_specs=[hbm, hbm, vmem, vmem, vmem],
        out_specs=(hbm, vmem, vmem),
        scratch_shapes=scratch,
        compiler_params=pltpu.CompilerParams(
            collective_id=0, has_side_effects=True, vmem_limit_bytes=44 * 1024 * 1024
        ),
        cost_estimate=pl.CostEstimate(flops=flops, bytes_accessed=6 * T * D, transcendentals=T * D),
    )(tokens[0], cotangent[0], conv_taps, block_mixes, gate_gain[None])
    mixes_grad = mixes.reshape(6, 2, T, LANES).transpose(0, 2, 1, 3).reshape(6, T, T).astype(F32) * mix_scale
    rows = small_sums[:, :, :4].transpose(2, 0, 1, 3).reshape(4, D) * tok_scale
    return input_grad[None], mixes_grad, rows[:3], rows[3]


def solution(mesh):
    placed = (P("dp", "seq", None), P("dp", "seq", None), P(), P(), P())
    return jax.shard_map(
        local,
        mesh=mesh,
        in_specs=placed,
        out_specs=(P("dp", "seq", None), P(), P(), P()),
        check_vma=False,
    )
```

time: 397 us -> 105 us (0.26)
  waiting for transfers between devices: 220 us -> 0 us
  blocking collectives: 107 us -> 0 us
  Pallas kernels: 0 us -> 96.1 us
  starting transfers between devices: 35.4 us -> 0 us
  between operations: 14.4 us -> 0.67 us
  matrix products: 10.5 us -> 0 us
  other arithmetic: 4.95 us -> 0.13 us
    psum x1 -> x0, waiting for transfers between devices: 172 us -> none  [local(): lax.psum((local_grads, taps_part, gain_part), ('dp', 'seq'))]
    psum x1 -> x0, blocking collectives: 107 us -> none  [local(): lax.psum((local_grads, taps_part, gain_part), ('dp', 'seq'))]
    pallas_call x0 -> x1, Pallas kernels: none -> 96.1 us  [local(): pl.pallas_call(kernel, out_shape=(jax.ShapeDtypeStruct((T, D), BF16), jax...]
    ppermute x8 -> x0, waiting for transfers between devices: 47.7 us -> none  [the longest x4 47.6 us: partner_2(): lax.ppermute(shard, axis, [(i, i ^ 1 << distance) for i in range(lax.axis...]
    ppermute x8 -> x0, starting transfers between devices: 35.4 us -> none  [the longest x4 25.2 us: partner_2(): lax.ppermute(shard, axis, [(i, i ^ 1 << distance) for i in range(lax.axis...]
    dot_general x18 -> x0, matrix products: 10.5 us -> none  [the longest x6 4.98 us: apply_mix(): jnp.einsum('ij,sjd->sid', matrix, block, preferred_element_type=jnp.float32)]
  transfers between devices with their start and end apart: 9 -> 0, of which waited for: 5 -> 0; matrix products, arithmetic and copies ran while one was open for 4% -> 0% of each run, Pallas kernels for 0% -> 0%
where the time goes in v1:
time: 105 us; the launch traced here: 104 us
  Pallas kernels  96.1 us (92%)
  local copies, waits for them, and re-layouts  7.61 us (7%)
    pallas_call x1, Pallas kernels, local(): pl.pallas_call(kernel, out_shape=(jax.ShapeDtypeStruct((T, D), BF16), jax...  96.1 us
    unnamed x11, local copies, waits for them, and re-layouts  4.99 us

profile of v1, /device:TPU:1, one launch (start us, length us, event | category | flops | bytes accessed | tf_op | source)
XLA Modules:
  0.0 104.5 jit_solution(10981448871438538308)
XLA Ops:
  0.6 0.7 broadcast_in_dim.6.gain_ref
  1.3 0.0 copy-start
  1.3 1.1 %copy-done = bf16[1,256,1536]{2,1,0:T(8,128)(2,1)S(1)} copy-done((bf16[1,256,1536]{2,1,0:T(8,128)(2,1)S(1)}, bf16[1,256,1536]{2,1,0:T(8,128)(2,1)}, u32[]{:S(2)}) %copy-start) | copy-done | bytes 786456
  2.5 0.0 copy-start.1
  2.5 1.1 %copy-done.1 = bf16[1,256,1536]{2,1,0:T(8,128)(2,1)S(1)} copy-done((bf16[1,256,1536]{2,1,0:T(8,128)(2,1)S(1)}, bf16[1,256,1536]{2,1,0:T(8,128)(2,1)}, u32[]{:S(2)}) %copy-start.1) | copy-done | bytes 786456
  3.6 0.0 copy-start.2
  3.6 1.1 %copy-done.2 = bf16[6,256,256]{2,1,0:T(8,128)(2,1)S(1)} copy-done((bf16[6,256,256]{2,1,0:T(8,128)(2,1)S(1)}, bf16[6,256,256]{2,1,0:T(8,128)(2,1)}, u32[]{:S(2)}) %copy-start.2) | copy-done | bytes 786456
  4.7 0.0 copy-start.3
  4.7 0.7 copy-done.3
  5.4 96.1 %shard_map.84 = (bf16[256,1536]{1,0:T(8,128)(2,1)S(1)}, bf16[3072,128]{1,0:T(8,128)(2,1)S(1)}, f32[4,3,8,128]{3,2,1,0:T(8,128)S(1)}) custom-call(bf16[256,1536]{1,0:T(8,128)(2,1)S(1)} %bitcast.15, bf16[256,1536]{1,0:T(8,128)(2,1)S(1)} %bitcast.16, bf16[3,1536]{1,0:T(4,128)(2,1)S(1)} %copy-done.3, bf16[6,256,256]{2,1,0:T(8,128)(2,1)S(1)} %copy-done.2, ...), custom_call_target="tpu_custom_call" | custom-call | flops 3623878656 | bytes 2359296 | tf_op jit(solution)/shard_map/pallas_call | solution.py:558
  101.5 0.0 copy-start.4
  101.6 0.6 squeeze.11
  102.2 0.1 convert_multiply_fusion
  102.3 1.3 %copy.12 = f32[6,2,32,8,128]{4,3,1,2,0:T(8,128)} copy(f32[6,2,32,8,128]{4,3,2,1,0:T(8,128)S(1)} %bitcast.17) | data formatting | bytes 3145728 | tf_op jit(solution)/shard_map/mul | solution.py:573
  103.6 0.0 copy-done.4
  103.6 0.9 copy.14
  (2 shorter events, 0.0 us)
Async XLA Ops:
  1.3 1.1 %copy-start = (bf16[1,256,1536]{2,1,0:T(8,128)(2,1)S(1)}, bf16[1,256,1536]{2,1,0:T(8,128)(2,1)}, u32[]{:S(2)}) copy-start(bf16[1,256,1536]{2,1,0:T(8,128)(2,1)} %param.5) | copy-start | bytes 2359300
  2.5 1.1 %copy-start.1 = (bf16[1,256,1536]{2,1,0:T(8,128)(2,1)S(1)}, bf16[1,256,1536]{2,1,0:T(8,128)(2,1)}, u32[]{:S(2)}) copy-start(bf16[1,256,1536]{2,1,0:T(8,128)(2,1)} %param.6) | copy-start | bytes 2359300
  3.6 1.1 %copy-start.2 = (bf16[6,256,256]{2,1,0:T(8,128)(2,1)S(1)}, bf16[6,256,256]{2,1,0:T(8,128)(2,1)}, u32[]{:S(2)}) copy-start(bf16[6,256,256]{2,1,0:T(8,128)(2,1)} %mixes_ref.1) | copy-start | bytes 2359300
  4.7 0.7 copy-start.3
  101.5 2.1 %copy-start.4 = (f32[4,4,3,128]{3,0,2,1:T(4,128)}, f32[4,4,3,128]{3,0,2,1:T(4,128)S(1)}, u32[]{:S(2)}) copy-start(f32[4,4,3,128]{3,0,2,1:T(4,128)S(1)} %multiply_bitcast_fusion) | copy-start | bytes 73732

commit v2 on v1

--- a/solution.py
+++ b/solution.py
@@ -21,6 +21,7 @@
 EDGE = 16
 TILE = 16
 ROWS = 6 * T * T // LANES
+REGIONS = (32, 16)
 HALF, PX, PY = ROWS // CORES, ROWS // (CORES * XS), ROWS // (CORES * XS * YS)
 
 
@@ -42,15 +43,15 @@
 
 
 def kernel(
-    tok_hbm, cot_hbm, taps_ref, mixes_ref, gain_ref,
+    tok_hbm, cot_hbm, taps_hbm, mixes_hbm, gain_ref,
     out_hbm, ag, e_out,
     tok, cot, halo, pad, conv, gf2, h, f2, t2, s2, gt, gs2, g1, fourth,
-    gcpad, ggg, outb, edge_out, edges, wts,
+    gcpad, ggg, outb, edge_out, edges, wts, taps_ref, mixes_ref,
     m0, m12, m3, m45, m0t, m12t, m3t, m45t,
-    grads, own_x, own_y, core_out, core_in, x_out, x_in, y_out, y_in, z_in,
+    grads, own_x, core_out, core_in, x_out, x_in, y_out, y_in, z_in,
     e_own, e_core, e_x, e_y, e_z,
-    in_send, in_recv, in_local, halo_send, halo_recv, edge_send, edge_recv,
-    out_send, out_recv, out_local, core_sem, x_send, x_recv, y_send, y_recv,
+    param_sem, in_send, in_recv, in_local, halo_send, halo_recv, edge_send, edge_recv,
+    out_send, out_recv, out_local, core_send, core_recv, x_send, x_recv, y_send, y_recv,
     z_send, z_recv, gy_send, gy_recv, gx_send, gx_recv, gc_send, gc_recv,
     ec_sem, ex_send, ex_recv, ey_send, ey_recv, ez_send, ez_recv, eq_send, eq_recv,
 ):
@@ -85,6 +86,13 @@
 
     def lanes(quarter, c):
         return pl.ds(pl.multiple_of(quarter * QUARTER + c * LANES, LANES), LANES)
+
+    params = [
+        pltpu.make_async_copy(src, dst, param_sem.at[i])
+        for i, (src, dst) in enumerate(((mixes_hbm, mixes_ref), (taps_hbm, taps_ref)))
+    ]
+    for copy in params:
+        copy.start()
 
     barrier = pltpu.get_barrier_semaphore()
     others = [in_group(yp, zp, m) for m in mates]
@@ -116,10 +124,10 @@
     for copy in halo_copies:
         copy.start()
 
-    def inbound(c, arrays=(0, 1)):
+    def inbound(c):
         copies = []
         for m in (1, 2, 0):
-            for a in arrays:
+            for a in range(2):
                 src, dst = ((tok_hbm, tok), (cot_hbm, cot))[a]
                 copies.append(
                     rcopy(
@@ -145,6 +153,8 @@
     def transposed(v):
         return v.astype(F32).T.astype(BF16)
 
+    for copy in params:
+        copy.wait()
     m0[...] = mixes_ref[0]
     m12[:, :T], m12[:, T:] = mixes_ref[1], mixes_ref[2]
     m3[...] = mixes_ref[3]
@@ -154,7 +164,8 @@
     m3t[...] = transposed(mixes_ref[3])
     m45t[:, :T], m45t[:, T:] = transposed(mixes_ref[4]), transposed(mixes_ref[5])
     wts[0:3, :] = taps_ref[...].astype(F32)
-    wts[3:4, :] = gain_ref[...]
+    for i in range(D // LANES):
+        wts[3:4, i * LANES : (i + 1) * LANES] = gain_ref[i : i + 1, :]
     grads[...] = jnp.zeros_like(grads)
     e_own[...] = jnp.zeros_like(e_own)
 
@@ -342,19 +353,17 @@
         ).wait_recv()
 
     def step(c, carry):
-        @pl.when(c > 0)
+        wait_inbound(c)
+        chain(c)
+
+        @pl.when(c < CHUNKS - 1)
         def _():
-            sums(c - 1)
-            finish(c - 1)
-
-        wait_inbound(c)
-
-        @pl.when(c == CHUNKS - 1)
+            sums(c)
+
+        @pl.when(c == CHUNKS - 2)
         def _():
-            for past in range(CHUNKS - 1):
-                send_out(past)
-
-        chain(c)
+            finish(0)
+
         return carry
 
     lax.fori_loop(0, CHUNKS, step, 0)
@@ -367,139 +376,213 @@
     def rows_of(start, size):
         return pl.ds(pl.multiple_of(start, EDGE), size)
 
-    core_out[...] = grads[rows_of((1 - core) * HALF, HALF), :].astype(BF16)
-    core_copy = rcopy(core_out, core_in, core_sem.at[0], core_sem.at[1], sibling)
-    core_copy.start()
+    sent = list(halo_copies)
+
+    def begin(copies):
+        for copy in copies:
+            copy.start()
+        sent.extend(copies)
+        return copies
+
+    def slot_wait(ref, slot, send, recv):
+        rcopy(ref.at[slot], ref.at[slot], send, recv, sibling).wait_recv()
+
+    def offset(r):
+        return CORES * XS * YS * sum(REGIONS[:r]) // CORES
+
+    def sizes(r):
+        return offset(r), YS * REGIONS[r], REGIONS[r]
+
+    def core_stage(r):
+        base, px, py = sizes(r)
+        there = pl.ds(base, XS * px)
+        core_out[there, :] = grads[rows_of((1 - core) * HALF + base, XS * px), :].astype(BF16)
+        return begin([rcopy(core_out.at[there], core_in.at[there], core_send.at[r], core_recv.at[r], sibling)])
+
+    def x_stage(r, copies):
+        base, px, py = sizes(r)
+        for copy in copies:
+            copy.wait_recv()
+        rows = pl.ds(base // XS, px)
+        started = []
+        for i, other in enumerate(x_mates):
+            part = grads[rows_of(core * HALF + base + other * px, px), :]
+            x_out[i, rows, :] = (part + core_in[rows_of(base + other * px, px), :].astype(F32)).astype(BF16)
+            started += begin(
+                [rcopy(x_out.at[i, rows], x_in.at[i, rows], x_send.at[r, i], x_recv.at[r, i], at(x_=other))]
+            )
+        part = grads[rows_of(core * HALF + base + x * px, px), :]
+        own_x[rows, :] = part + core_in[rows_of(base + x * px, px), :].astype(F32)
+        return started
+
+    def y_stage(r, copies):
+        base, px, py = sizes(r)
+        for copy in copies:
+            copy.wait_recv()
+        rows = pl.ds(base // XS, px)
+        own_x[rows, :] += sum(x_in[i, rows, :].astype(F32) for i in range(XS - 1))
+        y_out[rows, :] = own_x[rows, :].astype(BF16)
+        there = pl.ds(base // (XS * YS), py)
+        return begin(
+            [
+                rcopy(
+                    y_out.at[rows_of(base // XS + other * py, py)],
+                    y_in.at[i, there],
+                    y_send.at[r, i],
+                    y_recv.at[r, i],
+                    at(y_=other),
+                )
+                for i, other in enumerate(y_mates)
+            ]
+        )
+
+    def z_stage(r, copies):
+        base, px, py = sizes(r)
+        for copy in copies:
+            copy.wait_recv()
+        rows = pl.ds(base // (XS * YS), py)
+        total = own_x[rows_of(base // XS + y * py, py), :]
+        total = total + sum(y_in[i, rows, :].astype(F32) for i in range(YS - 1))
+        z_in[z, rows, :] = total.astype(BF16)
+        return begin(
+            [
+                rcopy(z_in.at[z, rows], z_in.at[z, rows], z_send.at[r, i], z_recv.at[r, i], at(z_=other))
+                for i, other in enumerate(z_mates)
+            ]
+        )
+
+    def gather_y(r):
+        base, px, py = sizes(r)
+        rows = pl.ds(base // (XS * YS), py)
+        for i in range(ZS - 1):
+            there = z_in.at[lax.rem(z + ZS - 1 - i, ZS), rows]
+            rcopy(there, there, z_send.at[r, i], z_recv.at[r, i], sibling).wait_recv()
+        total = z_in[0, rows, :].astype(F32)
+        for i in range(1, ZS):
+            total = total + z_in[i, rows, :].astype(F32)
+        own = rows_of(core * HALF + base + x * px + y * py, py)
+        ag[own, :] = total.astype(BF16)
+        begin(
+            [
+                rcopy(ag.at[own], ag.at[own], gy_send.at[r, i], gy_recv.at[r, i], at(y_=other))
+                for i, other in enumerate(y_mates)
+            ]
+        )
+
+    def gather_x(r):
+        base, px, py = sizes(r)
+        for i in range(YS - 1):
+            there = ag.at[rows_of(core * HALF + base + x * px + lax.rem(y + YS - 1 - i, YS) * py, py)]
+            rcopy(there, there, gy_send.at[r, i], gy_recv.at[r, i], sibling).wait_recv()
+        mine = ag.at[rows_of(core * HALF + base + x * px, px)]
+        begin(
+            [
+                rcopy(mine, mine, gx_send.at[r, i], gx_recv.at[r, i], at(x_=other))
+                for i, other in enumerate(x_mates)
+            ]
+            + [rcopy(mine, mine, gc_send.at[r, 0], gc_recv.at[r, 0], sibling)]
+        )
+
+    def gather_core(r):
+        base, px, py = sizes(r)
+        for i in range(XS - 1):
+            there = ag.at[rows_of(core * HALF + base + lax.rem(x + XS - 1 - i, XS) * px, px)]
+            rcopy(there, there, gx_send.at[r, i], gx_recv.at[r, i], sibling).wait_recv()
+            begin([rcopy(there, there, gc_send.at[r, i + 1], gc_recv.at[r, i + 1], sibling)])
+
+    def gather_end(r):
+        base, px, py = sizes(r)
+        for i in range(XS):
+            there = ag.at[rows_of((1 - core) * HALF + base + lax.rem(x + XS - i, XS) * px, px)]
+            rcopy(there, there, gc_send.at[r, i], gc_recv.at[r, i], sibling).wait_recv()
+
+    regions = range(len(REGIONS))
+    flights = [core_stage(r) for r in regions]
+    send_out(0)
     sums(CHUNKS - 1)
-    e_core_copy = rcopy(e_own, e_core, ec_sem.at[0], ec_sem.at[1], sibling)
-    e_core_copy.start()
-    core_copy.wait_recv()
-    x_copies = []
-    for i, other in enumerate(x_mates):
-        part = grads[rows_of(core * HALF + other * PX, PX), :] + core_in[rows_of(other * PX, PX), :].astype(F32)
-        x_out[i] = part.astype(BF16)
-        x_copies.append(rcopy(x_out.at[i], x_in.at[i], x_send.at[i], x_recv.at[i], at(x_=other)))
-        x_copies[-1].start()
-    own_x[...] = grads[rows_of(core * HALF + x * PX, PX), :] + core_in[rows_of(x * PX, PX), :].astype(F32)
-
+    e_core_copy = begin([rcopy(e_own, e_core, ec_sem.at[0], ec_sem.at[1], sibling)])[0]
+    flights = [x_stage(r, flights[r]) for r in regions]
+    for past in range(1, CHUNKS - 1):
+        finish(past)
+        send_out(past)
     e_core_copy.wait_recv()
     e_x[x] = e_own[...] + e_core[...]
-    ex_copies = [
-        rcopy(e_x.at[x], e_x.at[x], ex_send.at[i], ex_recv.at[i], at(x_=other)) for i, other in enumerate(x_mates)
-    ]
-    for copy in ex_copies:
-        copy.start()
-
+    begin(
+        [rcopy(e_x.at[x], e_x.at[x], ex_send.at[i], ex_recv.at[i], at(x_=other)) for i, other in enumerate(x_mates)]
+    )
     finish(CHUNKS - 1)
     send_out(CHUNKS - 1)
-
-    for copy in x_copies:
-        copy.wait_recv()
-    own_x[...] += x_in[0].astype(F32) + x_in[1].astype(F32) + x_in[2].astype(F32)
-    y_out[...] = own_x[...].astype(BF16)
-    y_copies = [
-        rcopy(y_out.at[rows_of(other * PY, PY)], y_in.at[i], y_send.at[i], y_recv.at[i], at(y_=other))
-        for i, other in enumerate(y_mates)
-    ]
-    for copy in y_copies:
-        copy.start()
-
-    def slot_wait(ref, slot, send, recv, device):
-        rcopy(ref.at[slot], ref.at[slot], send, recv, device).wait_recv()
+    flights = [y_stage(r, flights[r]) for r in regions]
 
     for i in range(XS - 1):
-        slot_wait(e_x, lax.rem(x + XS - 1 - i, XS), ex_send.at[i], ex_recv.at[i], sibling)
+        slot_wait(e_x, lax.rem(x + XS - 1 - i, XS), ex_send.at[i], ex_recv.at[i])
     e_y[yp] = e_x[0] + e_x[1] + e_x[2] + e_x[3]
-    ey_copies = [
-        rcopy(e_y.at[yp], e_y.at[yp], ey_send.at[i], ey_recv.at[i], at(y_=lax.rem(y + 2 * (i + 1), YS)))
-        for i in range(3)
-    ]
-    for copy in ey_copies:
-        copy.start()
-
-    for copy in y_copies:
-        copy.wait_recv()
-    total = own_x[rows_of(y * PY, PY), :]
-    for i in range(YS - 1):
-        total = total + y_in[i].astype(F32)
-    z_in[z] = total.astype(BF16)
-    z_copies = [
-        rcopy(z_in.at[z], z_in.at[z], z_send.at[i], z_recv.at[i], at(z_=other)) for i, other in enumerate(z_mates)
-    ]
-    for copy in z_copies:
-        copy.start()
+    begin(
+        [
+            rcopy(e_y.at[yp], e_y.at[yp], ey_send.at[i], ey_recv.at[i], at(y_=lax.rem(y + 2 * (i + 1), YS)))
+            for i in range(3)
+        ]
+    )
+    for r in regions:
+        z_stage(r, flights[r])
 
     for i in range(3):
-        slot_wait(e_y, lax.rem(yp + 3 - i, 4), ey_send.at[i], ey_recv.at[i], sibling)
+        slot_wait(e_y, lax.rem(yp + 3 - i, 4), ey_send.at[i], ey_recv.at[i])
     ez_me = z_hi * 2 + zp
     e_z[ez_me] = e_y[0] + e_y[1] + e_y[2] + e_y[3]
 
     def ez_device(slot):
         return at(z_=lax.div(slot, 2) * ZLO + 2 * zb + lax.rem(slot, 2))
 
-    ez_copies = [
-        rcopy(e_z.at[ez_me], e_z.at[ez_me], ez_send.at[i], ez_recv.at[i], ez_device(lax.rem(ez_me + i + 1, 4)))
-        for i in range(3)
-    ]
-    for copy in ez_copies:
-        copy.start()
-
-    for i in range(ZS - 1):
-        slot_wait(z_in, lax.rem(z + ZS - 1 - i, ZS), z_send.at[i], z_recv.at[i], sibling)
-    total = z_in[0].astype(F32)
-    for i in range(1, ZS):
-        total = total + z_in[i].astype(F32)
-    own = rows_of(core * HALF + x * PX + y * PY, PY)
-    ag[own, :] = total.astype(BF16)
-    gy_copies = [
-        rcopy(ag.at[own], ag.at[own], gy_send.at[i], gy_recv.at[i], at(y_=other)) for i, other in enumerate(y_mates)
-    ]
-    for copy in gy_copies:
-        copy.start()
+    begin(
+        [
+            rcopy(e_z.at[ez_me], e_z.at[ez_me], ez_send.at[i], ez_recv.at[i], ez_device(lax.rem(ez_me + i + 1, 4)))
+            for i in range(3)
+        ]
+    )
+    for r in regions:
+        gather_y(r)
 
     for i in range(3):
-        slot_wait(e_z, lax.rem(ez_me + 3 - i, 4), ez_send.at[i], ez_recv.at[i], sibling)
+        slot_wait(e_z, lax.rem(ez_me + 3 - i, 4), ez_send.at[i], ez_recv.at[i])
     e_out[q] = e_z[0] + e_z[1] + e_z[2] + e_z[3]
-    eq_copies = [
-        rcopy(e_out.at[q], e_out.at[q], eq_send.at[i], eq_recv.at[i], in_group(yp, zp, mates[i])) for i in range(3)
-    ]
-    for copy in eq_copies:
-        copy.start()
-
-    for i in range(YS - 1):
-        there = rows_of(core * HALF + x * PX + lax.rem(y + YS - 1 - i, YS) * PY, PY)
-        rcopy(ag.at[there], ag.at[there], gy_send.at[i], gy_recv.at[i], sibling).wait_recv()
-    mine = rows_of(core * HALF + x * PX, PX)
-    gx_copies = [
-        rcopy(ag.at[mine], ag.at[mine], gx_send.at[i], gx_recv.at[i], at(x_=other)) for i, other in enumerate(x_mates)
-    ]
-    for copy in gx_copies:
-        copy.start()
-    gc_copies = [rcopy(ag.at[mine], ag.at[mine], gc_send.at[0], gc_recv.at[0], sibling)]
-    gc_copies[0].start()
-    for i in range(XS - 1):
-        there = rows_of(core * HALF + lax.rem(x + XS - 1 - i, XS) * PX, PX)
-        rcopy(ag.at[there], ag.at[there], gx_send.at[i], gx_recv.at[i], sibling).wait_recv()
-        gc_copies.append(rcopy(ag.at[there], ag.at[there], gc_send.at[i + 1], gc_recv.at[i + 1], sibling))
-        gc_copies[-1].start()
+    begin(
+        [
+            rcopy(e_out.at[q], e_out.at[q], eq_send.at[i], eq_recv.at[i], in_group(yp, zp, mates[i]))
+            for i in range(3)
+        ]
+    )
+    for r in regions:
+        gather_x(r)
+    for r in regions:
+        gather_core(r)
 
     for i in range(3):
-        slot_wait(e_out, mates[2 - i], eq_send.at[i], eq_recv.at[i], sibling)
+        slot_wait(e_out, mates[2 - i], eq_send.at[i], eq_recv.at[i])
     for c in range(CHUNKS):
         for m in range(3):
             rcopy(
                 outb.at[c, mates[m]], out_hbm.at[:, lanes(mates[m], c)], out_send.at[c, m], out_recv.at[c, m], sibling
             ).wait_recv()
         out_own(c).wait()
-    for i in range(XS):
-        there = rows_of((1 - core) * HALF + lax.rem(x + XS - i, XS) * PX, PX)
-        rcopy(ag.at[there], ag.at[there], gc_send.at[i], gc_recv.at[i], sibling).wait_recv()
-    sent = halo_copies + [core_copy, e_core_copy] + x_copies + ex_copies + y_copies + ey_copies
-    sent += z_copies + ez_copies + gy_copies + eq_copies + gx_copies + gc_copies
+    for r in regions:
+        gather_end(r)
     for c in range(CHUNKS):
         sent += inbound(c) + edge_copies(c) + outbound(c)
     for copy in sent:
         copy.wait_send()
+
+
+def closing_kernel(grad_ref, ag_ref, small_ref, grad_out, mixes_out, taps_out, gain_out, *, mix_scale, tok_scale):
+    grad_out[...] = grad_ref[...]
+    for m in range(mixes_out.shape[0]):
+        for side in range(2):
+            part = ag_ref[(2 * m + side) * T : (2 * m + side + 1) * T, :].astype(F32)
+            mixes_out[m, :, side * LANES : (side + 1) * LANES] = part * mix_scale
+    for i in range(D // LANES):
+        part = small_ref[i // CHUNKS, i % CHUNKS] * tok_scale
+        taps_out[:, i * LANES : (i + 1) * LANES] = part[:3]
+        gain_out[i : i + 1, :] = part[3:4]
 
 
 def local(tokens, cotangent, conv_taps, block_mixes, gate_gain):
@@ -528,10 +611,11 @@
         pltpu.VMEM((CHUNKS, 4, T, LANES), BF16),
         *[pltpu.VMEM((CHUNKS, 4, EDGE, LANES), BF16)] * 2,
         pltpu.VMEM((8, D), F32),
+        pltpu.VMEM((3, D), BF16),
+        pltpu.VMEM((6, T, T), BF16),
         *[pltpu.VMEM((T, n * T), BF16) for n in (1, 2, 1, 2, 1, 2, 1, 2)],
         pltpu.VMEM((ROWS, LANES), F32),
         pltpu.VMEM((PX, LANES), F32),
-        pltpu.VMEM((PY, LANES), F32),
         *[pltpu.VMEM((HALF, LANES), BF16)] * 2,
         *[pltpu.VMEM((XS - 1, PX, LANES), BF16)] * 2,
         pltpu.VMEM((PX, LANES), BF16),
@@ -539,21 +623,22 @@
         pltpu.VMEM((ZS, PY, LANES), BF16),
         *[pltpu.VMEM(small, F32)] * 2,
         *[pltpu.VMEM((4, *small), F32)] * 3,
+        dma((2,)),
         *[dma((2, CHUNKS, 3))] * 2, dma((2, CHUNKS)),
         *[dma((4,))] * 2,
         *[dma((CHUNKS, 4))] * 2,
         *[dma((CHUNKS, 3))] * 2, dma((CHUNKS,)),
-        dma((2,)),
-        *[dma((XS - 1,))] * 2,
-        *[dma((YS - 1,))] * 2,
-        *[dma((ZS - 1,))] * 2,
-        *[dma((YS - 1,))] * 2,
-        *[dma((XS - 1,))] * 2,
-        *[dma((XS,))] * 2,
+        *[dma((len(REGIONS),))] * 2,
+        *[dma((len(REGIONS), XS - 1))] * 2,
+        *[dma((len(REGIONS), YS - 1))] * 2,
+        *[dma((len(REGIONS), ZS - 1))] * 2,
+        *[dma((len(REGIONS), YS - 1))] * 2,
+        *[dma((len(REGIONS), XS - 1))] * 2,
+        *[dma((len(REGIONS), XS))] * 2,
         dma((2,)),
         *[dma((3,))] * 8,
     ]
-    vmem, hbm = pl.BlockSpec(memory_space=pltpu.VMEM), pl.BlockSpec(memory_space=pl.ANY)
+    vmem, hbm = pl.BlockSpec(memory_space=pltpu.VMEM), pl.BlockSpec(memory_space=pltpu.HBM)
     flops = 18 * 2 * T * T * D
     input_grad, mixes, small_sums = pl.pallas_call(
         kernel,
@@ -562,17 +647,38 @@
             jax.ShapeDtypeStruct((ROWS, LANES), BF16),
             jax.ShapeDtypeStruct((4, *small), F32),
         ),
-        in_specs=[hbm, hbm, vmem, vmem, vmem],
-        out_specs=(hbm, vmem, vmem),
+        in_specs=[hbm, hbm, hbm, hbm, vmem],
+        out_specs=(pl.BlockSpec(memory_space=pl.ANY), vmem, vmem),
         scratch_shapes=scratch,
         compiler_params=pltpu.CompilerParams(
-            collective_id=0, has_side_effects=True, vmem_limit_bytes=44 * 1024 * 1024
+            collective_id=0, has_side_effects=True, vmem_limit_bytes=56 * 1024 * 1024
         ),
         cost_estimate=pl.CostEstimate(flops=flops, bytes_accessed=6 * T * D, transcendentals=T * D),
-    )(tokens[0], cotangent[0], conv_taps, block_mixes, gate_gain[None])
-    mixes_grad = mixes.reshape(6, 2, T, LANES).transpose(0, 2, 1, 3).reshape(6, T, T).astype(F32) * mix_scale
-    rows = small_sums[:, :, :4].transpose(2, 0, 1, 3).reshape(4, D) * tok_scale
-    return input_grad[None], mixes_grad, rows[:3], rows[3]
+    )(tokens[0], cotangent[0], conv_taps, block_mixes, gate_gain.reshape(D // LANES, LANES))
+    steps = 3
+    fixed = lambda shape: pl.BlockSpec(shape, lambda i: (0,) * len(shape))
+    input_grad, mixes_grad, taps_grad, gain_grad = pl.pallas_call(
+        functools.partial(closing_kernel, mix_scale=mix_scale, tok_scale=tok_scale),
+        grid=(steps,),
+        out_shape=(
+            jax.ShapeDtypeStruct((T, D), BF16),
+            jax.ShapeDtypeStruct((6, T, T), F32),
+            jax.ShapeDtypeStruct((3, D), F32),
+            jax.ShapeDtypeStruct((D // LANES, LANES), F32),
+        ),
+        in_specs=[
+            pl.BlockSpec((T, D // steps), lambda i: (0, i)),
+            pl.BlockSpec((ROWS // steps, LANES), lambda i: (i, 0)),
+            fixed((4, *small)),
+        ],
+        out_specs=(
+            pl.BlockSpec((T, D // steps), lambda i: (0, i)),
+            pl.BlockSpec((6 // steps, T, T), lambda i: (i, 0, 0)),
+            fixed((3, D)),
+            fixed((D // LANES, LANES)),
+        ),
+    )(input_grad, mixes, small_sums)
+    return input_grad[None], mixes_grad, taps_grad, gain_grad.reshape(D)
 
 
 def solution(mesh):

time: 105 us -> 96.9 us (0.923)
  local copies, waits for them, and re-layouts: 7.61 us -> 0 us
    unnamed x11 -> x0, local copies, waits for them, and re-layouts: 4.99 us -> none
    pallas_call x1, Pallas kernels: 96.1 us -> 92.5 us  [local(): pl.pallas_call(kernel, out_shape=(jax.ShapeDtypeStruct((T, D), BF16), jax...]
    pallas_call x0 -> x1, Pallas kernels: none -> 3.52 us  [local(): pl.pallas_call(functools.partial(closing_kernel, mix_scale=mix_scale, tok...]
    mul x1 -> x0, local copies, waits for them, and re-layouts: 1.28 us -> none  [local(): mixes.reshape(6, 2, T, LANES).transpose(0, 2, 1, 3).reshape(6, T, T)]
where the time goes in v2:
time: 96.9 us; the launch traced here: 96.6 us
  Pallas kernels  96 us (99%)
    pallas_call x1, Pallas kernels, local(): pl.pallas_call(kernel, out_shape=(jax.ShapeDtypeStruct((T, D), BF16), jax...  92.5 us
    pallas_call x1, Pallas kernels, local(): pl.pallas_call(functools.partial(closing_kernel, mix_scale=mix_scale, tok...  3.52 us

profile of v2, /device:TPU:1, one launch (start us, length us, event | category | flops | bytes accessed | tf_op | source)
XLA Modules:
  0.0 96.6 jit_solution(15962830318943377044)
XLA Ops:
  0.6 92.5 %shard_map.84 = (bf16[256,1536]{1,0:T(8,128)(2,1)}, bf16[3072,128]{1,0:T(8,128)(2,1)}, f32[4,3,8,128]{3,2,1,0:T(8,128)}) custom-call(bf16[256,1536]{1,0:T(8,128)(2,1)} %bitcast.5, bf16[256,1536]{1,0:T(8,128)(2,1)} %bitcast.6, bf16[3,1536]{1,0:T(4,128)(2,1)} %taps_hbm.1, bf16[6,256,256]{2,1,0:T(8,128)(2,1)} %mixes_hbm.1, f32[12,128]{1,0:T(8,128)} %bitcast.8), custom_call_target="tpu_custom_call" | custom-call | flops 3623878656 | bytes 2359296 | tf_op jit(solution)/shard_map/pallas_call | solution.py:643
  93.1 3.5 %shard_map.85 = (bf16[256,1536]{1,0:T(8,128)(2,1)}, f32[6,256,256]{2,1,0:T(8,128)}, f32[3,1536]{1,0:T(4,128)}, f32[12,128]{1,0:T(8,128)}) custom-call(bf16[256,1536]{1,0:T(8,128)(2,1)} %get-tuple-element.11.grad_ref, bf16[3072,128]{1,0:T(8,128)(2,1)} %get-tuple-element.12.ag_ref, f32[4,3,8,128]{3,2,1,0:T(8,128)} %get-tuple-element.13.small_ref), custom_call_target="tpu_custom_call" | custom-call | tf_op jit(solution)/shard_map/pallas_call | solution.py:660

commit v3 on v2

--- a/solution.py
+++ b/solution.py
@@ -121,8 +121,6 @@
         )
         for m in range(4)
     ]
-    for copy in halo_copies:
-        copy.start()
 
     def inbound(c):
         copies = []
@@ -147,7 +145,7 @@
         ]
 
     for c in range(CHUNKS):
-        for copy in inbound(c) + local(c):
+        for copy in inbound(c) + local(c) + (halo_copies if c == 0 else []):
             copy.start()
 
     def transposed(v):
@@ -228,16 +226,16 @@
 
     def chain(c):
         for b in range(4):
-            pad[8 : 8 + T, b * LANES : (b + 1) * LANES] = tok[c, b].astype(F32)
+            pad[c, 8 : 8 + T, b * LANES : (b + 1) * LANES] = tok[c, b].astype(F32)
         chunk = pl.ds(pl.multiple_of(c * LANES, LANES), LANES)
         ends = [halo[s, :, chunk].astype(F32) for s in range(4)]
         fill_edges(
-            pad, *mask_edges([ends[0][EDGE - 1 :], ends[1][EDGE - 1 :]], [ends[2][:1], ends[3][:1]])
+            pad.at[c], *mask_edges([ends[0][EDGE - 1 :], ends[1][EDGE - 1 :]], [ends[2][:1], ends[3][:1]])
         )
         w = weights(c)
 
         def before(i, carry):
-            prev, cur, nxt = window(pad, i)
+            prev, cur, nxt = window(pad.at[c], i)
             rows = tile_rows(i)
             conv[rows, :] = (w[0] * prev + w[1] * cur + w[2] * nxt).astype(BF16)
             up = jnp.concatenate([cot[c, b, rows, :] for b in range(4)], axis=1).astype(F32)
@@ -246,7 +244,7 @@
             gf = (up * gate * sig).astype(BF16)
             gf2[rows, :] = gf
             gf2[pl.ds(pl.multiple_of(T + i * TILE, TILE), TILE), :] = near(gf)
-            h[rows, :] = up * sig * (1.0 + gate * (1.0 - sig))
+            h[c, rows, :] = up * sig * (1.0 + gate * (1.0 - sig))
             return carry
 
         lax.fori_loop(0, T // TILE, before, 0)
@@ -261,7 +259,7 @@
         third = mm(m3[...], s2[...]).astype(BF16)
         t2[:T, :], t2[T:, :] = third, near(third)
         g1[...] = mm(m12t[...], gs2[...]).astype(BF16)
-        fourth[...] = mm(m45[...], t2[...])
+        fourth[c] = mm(m45[...], t2[...])
         gc = mm(m0t[...], g1[...]).astype(BF16)
         gcpad[c, 8 : 8 + T, :] = gc.astype(F32)
         for half in range(2):
@@ -289,9 +287,9 @@
         w = weights(c)
 
         def after(i, carry):
-            prev, cur, nxt = window(pad, i)
+            prev, cur, nxt = window(pad.at[c], i)
             rows = tile_rows(i)
-            gg = h[rows, :] * fourth[rows, :]
+            gg = h[c, rows, :] * fourth[c, rows, :]
             gc = gcpad[c, pl.ds(pl.multiple_of(8 + i * TILE, 8), TILE), :]
             ggg[c, rows, :] = gg * w[3]
 
@@ -355,14 +353,6 @@
     def step(c, carry):
         wait_inbound(c)
         chain(c)
-
-        @pl.when(c < CHUNKS - 1)
-        def _():
-            sums(c)
-
-        @pl.when(c == CHUNKS - 2)
-        def _():
-            finish(0)
 
         return carry
 
@@ -498,11 +488,11 @@
 
     regions = range(len(REGIONS))
     flights = [core_stage(r) for r in regions]
-    send_out(0)
-    sums(CHUNKS - 1)
+    for c in range(CHUNKS):
+        sums(c)
     e_core_copy = begin([rcopy(e_own, e_core, ec_sem.at[0], ec_sem.at[1], sibling)])[0]
     flights = [x_stage(r, flights[r]) for r in regions]
-    for past in range(1, CHUNKS - 1):
+    for past in range(CHUNKS - 1):
         finish(past)
         send_out(past)
     e_core_copy.wait_recv()
@@ -511,7 +501,6 @@
         [rcopy(e_x.at[x], e_x.at[x], ex_send.at[i], ex_recv.at[i], at(x_=other)) for i, other in enumerate(x_mates)]
     )
     finish(CHUNKS - 1)
-    send_out(CHUNKS - 1)
     flights = [y_stage(r, flights[r]) for r in regions]
 
     for i in range(XS - 1):
@@ -525,6 +514,7 @@
     )
     for r in regions:
         z_stage(r, flights[r])
+    send_out(CHUNKS - 1)
 
     for i in range(3):
         slot_wait(e_y, lax.rem(yp + 3 - i, 4), ey_send.at[i], ey_recv.at[i])
@@ -595,17 +585,17 @@
     scratch = [
         *[pltpu.VMEM((CHUNKS, 4, T, LANES), BF16)] * 2,
         pltpu.VMEM((4, EDGE, QUARTER), BF16),
-        pltpu.VMEM((T + 16, WIDE), F32),
+        pltpu.VMEM((CHUNKS, T + 16, WIDE), F32),
         pltpu.VMEM(wide, BF16),
         pltpu.VMEM((2 * T, WIDE), BF16),
-        pltpu.VMEM(wide, F32),
+        pltpu.VMEM((CHUNKS, *wide), F32),
         pltpu.VMEM((2 * T, WIDE), BF16),
         pltpu.VMEM((2 * T, WIDE), BF16),
         pltpu.VMEM(wide, BF16),
         pltpu.VMEM(wide, BF16),
         pltpu.VMEM((2 * T, WIDE), BF16),
         pltpu.VMEM(wide, BF16),
-        pltpu.VMEM(wide, F32),
+        pltpu.VMEM((CHUNKS, *wide), F32),
         pltpu.VMEM((CHUNKS, T + 16, WIDE), F32),
         pltpu.VMEM((CHUNKS, T, WIDE), F32),
         pltpu.VMEM((CHUNKS, 4, T, LANES), BF16),
@@ -655,7 +645,7 @@
         ),
         cost_estimate=pl.CostEstimate(flops=flops, bytes_accessed=6 * T * D, transcendentals=T * D),
     )(tokens[0], cotangent[0], conv_taps, block_mixes, gate_gain.reshape(D // LANES, LANES))
-    steps = 3
+    steps = 2
     fixed = lambda shape: pl.BlockSpec(shape, lambda i: (0,) * len(shape))
     input_grad, mixes_grad, taps_grad, gain_grad = pl.pallas_call(
         functools.partial(closing_kernel, mix_scale=mix_scale, tok_scale=tok_scale),

time: 96.9 us -> 94.5 us (0.975)
  Pallas kernels: 96 us -> 93.7 us
    pallas_call x1, Pallas kernels: 92.5 us -> 91.1 us  [local(): pl.pallas_call(kernel, out_shape=(jax.ShapeDtypeStruct((T, D), BF16), jax...]
where the time goes in v3:
time: 94.5 us; the launch traced here: 94.3 us
  Pallas kernels  93.7 us (99%)
    pallas_call x1, Pallas kernels, local(): pl.pallas_call(kernel, out_shape=(jax.ShapeDtypeStruct((T, D), BF16), jax...  91.1 us
    pallas_call x1, Pallas kernels, local(): pl.pallas_call(functools.partial(closing_kernel, mix_scale=mix_scale, tok...  2.6 us

profile of v3, /device:TPU:1, one launch (start us, length us, event | category | flops | bytes accessed | tf_op | source)
XLA Modules:
  0.0 94.3 jit_solution(4299010919570426642)
XLA Ops:
  0.6 91.1 %shard_map.84 = (bf16[256,1536]{1,0:T(8,128)(2,1)}, bf16[3072,128]{1,0:T(8,128)(2,1)}, f32[4,3,8,128]{3,2,1,0:T(8,128)}) custom-call(bf16[256,1536]{1,0:T(8,128)(2,1)} %bitcast.5, bf16[256,1536]{1,0:T(8,128)(2,1)} %bitcast.6, bf16[3,1536]{1,0:T(4,128)(2,1)} %taps_hbm.1, bf16[6,256,256]{2,1,0:T(8,128)(2,1)} %mixes_hbm.1, f32[12,128]{1,0:T(8,128)} %bitcast.8), custom_call_target="tpu_custom_call" | custom-call | flops 3623878656 | bytes 2359296 | tf_op jit(solution)/shard_map/pallas_call | solution.py:633
  91.7 2.6 %shard_map.85 = (bf16[256,1536]{1,0:T(8,128)(2,1)}, f32[6,256,256]{2,1,0:T(8,128)}, f32[3,1536]{1,0:T(4,128)}, f32[12,128]{1,0:T(8,128)}) custom-call(bf16[256,1536]{1,0:T(8,128)(2,1)} %get-tuple-element.11.grad_ref, bf16[3072,128]{1,0:T(8,128)(2,1)} %get-tuple-element.12.ag_ref, f32[4,3,8,128]{3,2,1,0:T(8,128)} %get-tuple-element.13.small_ref), custom_call_target="tpu_custom_call" | custom-call | tf_op jit(solution)/shard_map/pallas_call | solution.py:650

commit v4 on v3

--- a/solution.py
+++ b/solution.py
@@ -21,7 +21,7 @@
 EDGE = 16
 TILE = 16
 ROWS = 6 * T * T // LANES
-REGIONS = (32, 16)
+REGIONS = (16, 16, 16)
 HALF, PX, PY = ROWS // CORES, ROWS // (CORES * XS), ROWS // (CORES * XS * YS)
 
 
@@ -95,7 +95,7 @@
         copy.start()
 
     barrier = pltpu.get_barrier_semaphore()
-    others = [in_group(yp, zp, m) for m in mates]
+    others = [in_group(yp, zp, 3 - q)]
     others += [in_group(next_yp, next_zp, m) for m in range(4)]
     others += [in_group(prev_yp, prev_zp, m) for m in range(4)]
     others += [at(core_=1 - core)]

time: 94.5 us -> 93.9 us (level)
  no operation moved by 1% of the time
where the time goes in v4:
time: 93.9 us; the launch traced here: 93.7 us
  Pallas kernels  93.1 us (99%)
    pallas_call x1, Pallas kernels, local(): pl.pallas_call(kernel, out_shape=(jax.ShapeDtypeStruct((T, D), BF16), jax...  90.5 us
    pallas_call x1, Pallas kernels, local(): pl.pallas_call(functools.partial(closing_kernel, mix_scale=mix_scale, tok...  2.6 us

profile of v4, /device:TPU:1, one launch (start us, length us, event | category | flops | bytes accessed | tf_op | source)
XLA Modules:
  0.0 93.7 jit_solution(17017202958882392346)
XLA Ops:
  0.6 90.5 %shard_map.84 = (bf16[256,1536]{1,0:T(8,128)(2,1)}, bf16[3072,128]{1,0:T(8,128)(2,1)}, f32[4,3,8,128]{3,2,1,0:T(8,128)}) custom-call(bf16[256,1536]{1,0:T(8,128)(2,1)} %bitcast.5, bf16[256,1536]{1,0:T(8,128)(2,1)} %bitcast.6, bf16[3,1536]{1,0:T(4,128)(2,1)} %taps_hbm.1, bf16[6,256,256]{2,1,0:T(8,128)(2,1)} %mixes_hbm.1, f32[12,128]{1,0:T(8,128)} %bitcast.8), custom_call_target="tpu_custom_call" | custom-call | flops 3623878656 | bytes 2359296 | tf_op jit(solution)/shard_map/pallas_call | solution.py:633
  91.1 2.6 %shard_map.85 = (bf16[256,1536]{1,0:T(8,128)(2,1)}, f32[6,256,256]{2,1,0:T(8,128)}, f32[3,1536]{1,0:T(4,128)}, f32[12,128]{1,0:T(8,128)}) custom-call(bf16[256,1536]{1,0:T(8,128)(2,1)} %get-tuple-element.11.grad_ref, bf16[3072,128]{1,0:T(8,128)(2,1)} %get-tuple-element.12.ag_ref, f32[4,3,8,128]{3,2,1,0:T(8,128)} %get-tuple-element.13.small_ref), custom_call_target="tpu_custom_call" | custom-call | tf_op jit(solution)/shard_map/pallas_call | solution.py:650
